TPU v7x, 32 devices: a whole 2x2x4 slice. The times are simulated.
32 devices in a mesh: dom: 8 (over z, core), sub: 4 (over y, x).
Axes of the slice: x: 2, y: 2, z: 4, core: 2. Of those that a mesh axis runs over, the one named last changes fastest.
Arguments:
- modal_state: float32 [56, 9, 4096], P(None, None, ('dom', 'sub')), may hold values from -6 to 6
- stiffness: float32 [3, 56, 56], replicated, may hold values from -0.75 to 0.75
- jacobians: float32 [3, 9, 9, 4096], P(None, None, None, ('dom', 'sub')), may hold values from -1.25 to 1.25
- flux_solvers: float32 [2, 4, 9, 9, 4096], P(None, None, None, None, ('dom', 'sub')), may hold values from -0.75 to 0.75
- projector: float32 [4, 21, 56], replicated, may hold values from -0.75 to 0.75
- rotations: float32 [3, 21, 21], replicated, may hold values from -1.25 to 1.25
- yield_stress: float32 [4096], P(('dom', 'sub')), may hold values from 0.5 to 8
- cluster: int32 [4096], P(('dom', 'sub')), may hold values from 0 to 1
- orient: int32 [4, 4096], P(None, ('dom', 'sub')), may hold values from 0 to 2
- neighbour_slot: int32 [4, 4096], P(None, ('dom', 'sub')), may hold values from 0 to 703, as said below
- send_map: int32 [6144], P(('dom', 'sub')), may hold values from 0 to 511, as said below
Outputs:
- updated: float32 [56, 9, 4096], P(None, None, ('dom', 'sub'))
Inputs may be any that keep to these rules, and one draw needn't show every extreme that they name: `neighbour_slot`: within one partition every received slot 512 + r is named by exactly one face; the other faces name local faces. `send_map`: the 192 entries of one partition are distinct local face numbers.
All inputs are finite; a program needn't handle non-finite values.
Results may differ from a plain program's by a relative error of at most 0.0003.
Values sent between devices are 32-bit elements; how exact they have to be, the bound alone decides.
No kernel may reach another device: no remote copies, remote signals or barrier semaphores. Data moves between devices by JAX's collectives and lax.ppermute only.
A program may use at most 64 MiB of HBM per device.

v0:
```python
import math

import jax
import jax.numpy as jnp
from jax import lax
from jax.experimental import pallas as pl
from jax.experimental.pallas import tpu as pltpu
from jax.sharding import PartitionSpec as P

ORDER = 6
SLOTS_DOM = 64
SLOTS_SUB = 32
ROWS = 24
GROUP = 3

F32 = jnp.float32
BF16 = jnp.bfloat16
EXACT = lax.Precision.HIGHEST

DOM_GROUPS = ((0, 5), (5, 4))
SUB_GROUPS = ((0, 3), (3, 2), (5, 2), (7, 2))
PACKING = (DOM_GROUPS, DOM_GROUPS, SUB_GROUPS, SUB_GROUPS)

SUB_ROWS = SUB_GROUPS[0][1] * ROWS

FIRST_TURNS = (1, 0)
SECOND_TURNS = (1, 0)


INPUTS = 11
FIRST_USED = 5


def iota(shape, dim):
    return lax.broadcasted_iota(jnp.int32, shape, dim)


def dot(a, b):
    return jnp.dot(a, b, preferred_element_type=F32)


def exact_dot(a, b):
    return jnp.dot(a, b, precision=EXACT, preferred_element_type=F32)


def halves(value):
    high = value.astype(BF16)
    return high, (value - high.astype(F32)).astype(BF16)


def one_hot(index_row, first, count, modulus=None):
    number = iota((count, index_row.shape[1]), 0)
    if modulus is not None:
        number = lax.rem(number, modulus)
    return jnp.where(number + first == index_row, 1.0, 0.0).astype(BF16)


def fold_step(basis):
    return -(-basis // 16) * 16


def fold_rows(value):
    basis, lanes = value.shape
    rest = jnp.zeros((fold_step(basis) - basis, lanes), F32)
    value = jnp.concatenate([value, rest], axis=0)
    high, low = halves(value)
    return jnp.concatenate([high, high, low], axis=0)


def fold_columns(matrix):
    basis = matrix.shape[1]
    step = fold_step(basis)
    high, low = halves(matrix)
    row, column = iota((basis, 3 * step), 0), iota((basis, 3 * step), 1)
    outer = jnp.where((column == row) | (column == row + 2 * step), 1.0, 0.0).astype(BF16)
    inner = jnp.where(column == row + step, 1.0, 0.0).astype(BF16)
    return (dot(high, outer) + dot(low, inner)).astype(BF16)


def stiffen(stiff_fold, values, target, start, lanes):
    folded = jnp.concatenate([fold_rows(value) for value in values], axis=1)
    target[:, start * lanes:(start + len(values)) * lanes] = dot(stiff_fold, folded)


def mix_jacobians(stiffened, jac, basis, quants, lanes, take):
    for start in range(0, quants, GROUP):
        totals = [None] * GROUP
        for q in range(quants):
            for d in range(3):
                block = stiffened[d * basis:(d + 1) * basis, q * lanes:(q + 1) * lanes]
                for i in range(GROUP):
                    term = block * jac[q, start + i, d:d + 1, :]
                    totals[i] = term if totals[i] is None else totals[i] + term
        take(start, totals)


def mix_faces(table, flux, side, start, quants, lanes):
    totals = [[] for _ in range(GROUP)]
    for f in range(4):
        blocks = [
            table[q * ROWS:(q + 1) * ROWS, f * lanes:(f + 1) * lanes] for q in range(quants)
        ]
        for i in range(GROUP):
            total = blocks[0] * flux[side, 0, start + i, f:f + 1, :]
            for q in range(1, quants):
                total = total + blocks[q] * flux[side, q, start + i, f:f + 1, :]
            totals[i].append(total)
    return [jnp.concatenate(total, axis=0) for total in totals]


def fill_projector(projector, padded):
    modes, faces, basis = projector.shape
    padded[...] = jnp.zeros(padded.shape, F32)
    for f in range(faces):
        for m in range(modes):
            padded[f * ROWS + m:f * ROWS + m + 1, 0:basis] = projector[m, f:f + 1, :]


def predict(stiff_fold, jac, state, stiffened, first, second, basis, quants, lanes):
    for start in range(0, quants, GROUP):
        values = [state(q) for q in range(start, start + GROUP)]
        stiffen(stiff_fold, values, stiffened.at[0], start, lanes)
    for order in range(1, ORDER):
        factor = 1.0 / math.factorial(order + 1)

        def take(start, totals):
            if order + 1 < ORDER:
                stiffen(stiff_fold, totals, stiffened.at[order % 2], start, lanes)
            for p, total in enumerate(totals, start):
                first[p] = first[p] + factor * total
                if second is not None:
                    second[p] = second[p] + (2.0 ** (order + 1) - 1.0) * factor * total

        mix_jacobians(stiffened.at[(order - 1) % 2], jac, basis, quants, lanes, take)


def project_table(padded, field, table, basis, quants, lanes):
    fold = fold_columns(padded[:, 0:basis])
    for start in range(0, quants, GROUP):
        values = [fold_rows(field(q)) for q in range(start, start + GROUP)]
        flat = dot(fold, jnp.concatenate(values, axis=1))
        for q in range(start, start + GROUP):
            for f in range(4):
                table[q * ROWS:(q + 1) * ROWS, f * lanes:(f + 1) * lanes] = flat[
                    f * ROWS:(f + 1) * ROWS, (q - start) * lanes:(q - start + 1) * lanes
                ]


def even_spot():
    return [lax.rem(lax.axis_index(axis), 2) == 0 for axis in ("dom", "sub")]


def send_choice(send_row, faces, lanes):
    low = jnp.broadcast_to(send_row[:, 0:lanes], (8, lanes))
    lane = iota((8, lanes), 1)
    turned = pltpu.roll(low, SLOTS_DOM, 1)
    high = send_row[:, 2 * SLOTS_DOM:2 * SLOTS_DOM + 2 * SLOTS_SUB]
    spread = jnp.broadcast_to(jnp.concatenate([high, high], axis=1), (8, lanes))
    moved = pltpu.roll(spread, SLOTS_SUB, 1)
    left = lax.rem(lane, 2 * SLOTS_SUB) < SLOTS_SUB
    pieces = [
        jnp.where(lane < SLOTS_DOM, low, turned),
        jnp.where(lane < SLOTS_DOM, turned, low),
        jnp.where(left, spread, moved),
        jnp.where(left, moved, spread),
    ]
    even_dom, even_sub = even_spot()
    pieces = [
        jnp.where(even_dom, pieces[1], pieces[0]),
        jnp.where(even_dom, pieces[0], pieces[1]),
        jnp.where(even_sub, pieces[3], pieces[2]),
        jnp.where(even_sub, pieces[2], pieces[3]),
    ]
    return one_hot(jnp.concatenate([piece[0:1] for piece in pieces], axis=1), 0, faces)


def pick_sends(table, chosen, outs, turns, lanes):
    upper, lower = halves(table[...])
    sent = dot(upper, chosen) + dot(lower, chosen)
    for k, groups in enumerate(PACKING):
        out = outs[turns.index(k)] if k < 2 else outs[2]
        row = SUB_ROWS if k == 3 else 0
        width = lanes // len(groups)
        values = sent[:, k * lanes:(k + 1) * lanes]
        start, count = groups[0]
        packed = values[0:count * ROWS]
        least = min(count for _, count in groups) * ROWS
        spot = iota((least, lanes), 1)
        head = packed[0:least]
        for g, (start, _) in enumerate(groups):
            if g:
                head = jnp.where(
                    spot >= g * width, values[start * ROWS:start * ROWS + least], head
                )
        out[row:row + least] = head
        out[row + least:row + count * ROWS] = packed[least:]


def spread_received(arrived, groups, lanes):
    width = lanes // len(groups)
    parts = []
    for g, (_, count) in enumerate(groups):
        place = iota((count * ROWS, lanes), 1)
        mine = (place >= g * width) & (place < (g + 1) * width)
        parts.append(jnp.where(mine, arrived[0:count * ROWS], 0.0))
    return jnp.concatenate(parts, axis=0)


def pick_local(table, slot, faces):
    chosen = jnp.concatenate([one_hot(slot[f:f + 1], 0, faces) for f in range(4)], axis=1)
    upper, lower = halves(table)
    return dot(upper, chosen) + dot(lower, chosen)


def received_choice(slot, faces, lanes):
    even_dom, even_sub = even_spot()
    starts = (
        jnp.where(even_dom, faces + SLOTS_DOM, faces),
        jnp.where(even_dom, faces, faces + SLOTS_DOM),
        faces + 2 * SLOTS_DOM + jnp.where(even_sub, SLOTS_SUB, 0),
        faces + 2 * SLOTS_DOM + jnp.where(even_sub, 0, SLOTS_SUB),
    )
    widths = (SLOTS_DOM, SLOTS_DOM, SLOTS_SUB, SLOTS_SUB)
    return jnp.concatenate(
        [
            jnp.concatenate(
                [one_hot(slot[f:f + 1], first, lanes, width) for f in range(4)], axis=1
            )
            for first, width in zip(starts, widths)
        ],
        axis=0,
    )


def pick_received(doms, near, far, chosen, lanes):
    spot, count = lax.axis_index("sub"), lax.axis_size("sub")
    met = jnp.where(lax.rem(spot, 2) == 0, spot > 0, spot < count - 1)
    pieces = [
        doms[0][...],
        doms[1][...],
        near[0:SUB_ROWS],
        jnp.where(met, far[...], 0.0),
    ]
    spread = jnp.concatenate(
        [spread_received(item, groups, lanes) for item, groups in zip(pieces, PACKING)],
        axis=1,
    )
    upper, lower = halves(spread)
    return dot(upper, chosen) + dot(lower, chosen)


def lift(upper, lower, high, low):
    return dot(upper, high) + dot(lower, high) + dot(upper, low)


def local_update(
    base, integral, table, jac, turned_fold, flux, lifting, stiffened, part,
    basis, quants, lanes,
):
    for start in range(0, quants, GROUP):
        values = [integral(q) for q in range(start, start + GROUP)]
        stiffen(turned_fold, values, stiffened, start, lanes)
    upper, lower = halves(lifting)
    for start in range(0, quants, GROUP):
        solved = mix_faces(table, flux, 0, start, quants, lanes)
        high, low = halves(jnp.concatenate(solved, axis=1))
        own = lift(upper, lower, high, low)
        for i in range(GROUP):
            part[start + i] = base(start + i) - own[:, i * lanes:(i + 1) * lanes]

    def take(start, totals):
        for p, total in enumerate(totals, start):
            part[p] = part[p] + total

    mix_jacobians(stiffened, jac, basis, quants, lanes, take)


def near_lift(picked, flux, orient, lifting, quants, lanes, take):
    upper, lower = halves(lifting)
    masks = [
        jnp.concatenate(
            [
                jnp.broadcast_to(jnp.where(orient[f:f + 1] == o, 1.0, 0.0), (ROWS, lanes))
                for f in range(4)
            ],
            axis=0,
        ).astype(BF16)
        for o in range(3)
    ]
    for start in range(0, quants, GROUP):
        highs, lows = [], []
        for solved in mix_faces(picked, flux, 1, start, quants, lanes):
            high, low = halves(solved)
            highs.append(jnp.concatenate([high * mask for mask in masks], axis=0))
            lows.append(jnp.concatenate([low * mask for mask in masks], axis=0))
        near = lift(
            upper, lower, jnp.concatenate(highs, axis=1), jnp.concatenate(lows, axis=1)
        )
        for i in range(GROUP):
            take(start + i, near[:, i * lanes:(i + 1) * lanes])


def near_lifting(own_lifting, rotations):
    count, modes, _ = rotations.shape
    block = 4 * ROWS
    row, column = iota((modes, count * block), 0), iota((modes, count * block), 1)
    turned = jnp.zeros((modes, count * block), F32)
    for o in range(count):
        spot = (lax.rem(column, ROWS) == row) & (lax.div(column, block) == o)
        turned = turned + exact_dot(rotations[o], jnp.where(spot, 1.0, 0.0))
    row, column = iota((block, modes), 0), iota((block, modes), 1)
    tall = exact_dot(jnp.where(lax.rem(row, ROWS) == column, 1.0, 0.0), turned)
    row, column = iota(tall.shape, 0), iota(tall.shape, 1)
    same = lax.div(row, ROWS) == lax.div(lax.rem(column, block), ROWS)
    return exact_dot(own_lifting, jnp.where(same, tall, 0.0))


def first_kernel(*refs):
    inputs, refs = refs[:INPUTS], refs[INPUTS:]
    held, refs = refs[:INPUTS], refs[INPUTS:]
    first, second, table, padded, stiff_fold, choice, *sends, stiffened, arrivals = refs
    copies = [
        pltpu.make_async_copy(source, target, arrivals.at[k])
        for k, (source, target) in enumerate(zip(inputs, held))
    ]
    for copy in copies:
        copy.start()
    send_row, projector, stiffness, state, jac = held[:FIRST_USED]
    quants, basis, lanes = state.shape
    copies[0].wait()
    choice[...] = send_choice(send_row, 4 * lanes, lanes)
    copies[1].wait()
    fill_projector(projector, padded)
    copies[2].wait()
    fold = fold_columns(jnp.concatenate([stiffness[d] for d in range(3)], axis=0))
    stiff_fold[...] = fold.astype(F32)
    copies[3].wait()
    for q in range(quants):
        value = state[q]
        first[q] = value
        second[q] = value
    copies[4].wait()
    predict(
        fold, jac, lambda q: state[q], stiffened, first, second, basis, quants, lanes
    )
    project_table(padded, lambda q: first[q], table, basis, quants, lanes)
    pick_sends(table, choice[...], sends, FIRST_TURNS, lanes)
    for copy in copies[FIRST_USED:]:
        copy.wait()


def second_kernel(
    state, first, table, jac, stiffness, padded, rotations, flux, slot,
    part, picked, lifting, turned_fold, choice,
    stiffened,
):
    quants, basis, lanes = state.shape
    turned = jnp.concatenate([stiffness[d].T for d in range(3)], axis=0)
    fold = fold_columns(turned)
    turned_fold[...] = fold.astype(F32)
    own_lifting = padded[...].T[0:basis]
    lifting[...] = near_lifting(own_lifting, rotations)
    picked[...] = pick_local(table[...], slot, 4 * lanes)
    choice[...] = received_choice(slot, 4 * lanes, lanes)
    local_update(
        lambda p: state[p], lambda q: first[q], table, jac, fold, flux, own_lifting,
        stiffened, part, basis, quants, lanes,
    )


def third_kernel(
    state, first, second, part, picked_local, dom_a, dom_b, sub_near, sub_far,
    jac, stiff_fold, padded, flux, orient, cluster, lifting, received, choice,
    middle, integral, picked, table, *refs,
):
    *sends, stiffened = refs
    quants, basis, lanes = state.shape
    doms = [(dom_a, dom_b)[FIRST_TURNS.index(k)] for k in (0, 1)]
    picked[...] = picked_local[...] + pick_received(
        doms, sub_near, sub_far, received[...], lanes
    )
    fine = cluster[...] == 0

    def take(p, near):
        value = jnp.where(fine, part[p] - near, state[p])
        middle[p] = value
        integral[p] = value

    near_lift(picked, flux, orient, lifting[...], quants, lanes, take)
    predict(
        stiff_fold[...].astype(BF16), jac, lambda q: middle[q], stiffened, integral, None,
        basis, quants, lanes,
    )
    project_table(
        padded, lambda q: jnp.where(fine, integral[q], second[q]), table, basis, quants, lanes
    )
    for q in range(quants):
        integral[q] = jnp.where(fine, integral[q], first[q] + second[q])
    pick_sends(table, choice[...], sends, SECOND_TURNS, lanes)


def fourth_kernel(
    middle, integral, table_one, table_two, picked_one, jac, turned_fold, padded, flux, slot,
    cluster,
    part, picked,
    stiffened, total_table,
):
    quants, basis, lanes = middle.shape
    own_lifting = padded[...].T[0:basis]
    coarse = jnp.concatenate([cluster[...] != 0] * 4, axis=1)
    total_table[...] = table_two[...] + jnp.where(coarse, table_one[...], 0.0)
    picked[...] = pick_local(table_two[...], slot, 4 * lanes) + jnp.where(
        coarse, picked_one[...], 0.0
    )
    local_update(
        lambda p: middle[p], lambda q: integral[q], total_table, jac,
        turned_fold[...].astype(BF16), flux, own_lifting,
        stiffened, part, basis, quants, lanes,
    )


def fifth_kernel(
    part, picked_local, dom_a, dom_b, sub_near, sub_far, flux, orient, lifting, received,
    yield_stress,
    updated,
    picked,
):
    quants, basis, lanes = part.shape
    doms = [(dom_a, dom_b)[SECOND_TURNS.index(k)] for k in (0, 1)]
    picked[...] = picked_local[...] + pick_received(
        doms, sub_near, sub_far, received[...], lanes
    )
    stepped = [None] * quants

    def take(p, near):
        stepped[p] = part[p] - near

    near_lift(picked, flux, orient, lifting[...], quants, lanes, take)
    mean_part = (stepped[0] + stepped[1] + stepped[2]) / 3.0
    spread = [stepped[q] - mean_part for q in range(3)]
    normal = [item[0:1] for item in spread]
    shear = [stepped[q][0:1] for q in range(3, 6)]
    second_inv = 0.5 * (normal[0] ** 2 + normal[1] ** 2 + normal[2] ** 2) + (
        shear[0] ** 2 + shear[1] ** 2 + shear[2] ** 2
    )
    limit = yield_stress[...]
    scaling = limit / jnp.maximum(jnp.sqrt(second_inv), limit)
    for q in range(3):
        updated[q] = mean_part + scaling * spread[q]
    for q in range(3, 6):
        updated[q] = scaling * stepped[q]
    for q in range(6, quants):
        updated[q] = stepped[q]


def run(body, outs, scratch, *operands, space=pltpu.VMEM):
    vmem = pl.BlockSpec(memory_space=pltpu.VMEM)
    return pl.pallas_call(
        body,
        out_shape=[
            out if isinstance(out, jax.ShapeDtypeStruct) else jax.ShapeDtypeStruct(out, F32)
            for out in outs
        ],
        in_specs=[pl.BlockSpec(memory_space=space)] * len(operands),
        out_specs=[vmem] * len(outs),
        scratch_shapes=scratch,
        compiler_params=pltpu.CompilerParams(vmem_limit_bytes=32 * 1024 * 1024),
        name=body.__name__,
    )(*operands)


def hand_on(near, dom, onward):
    onward[...] = near[SUB_ROWS:2 * SUB_ROWS]


def exchange(sends, turns):
    def swap(value, axis, first):
        lower = range(first, lax.axis_size(axis) - 1, 2)
        return lax.ppermute(
            value, axis, [(i, i + 1) for i in lower] + [(i + 1, i) for i in lower]
        )

    count = lax.axis_size("sub")
    near = swap(sends[2], "sub", 0)
    doms = [swap(value, "dom", first) for value, first in zip(sends, turns)]
    kept, = run(hand_on, [(SUB_ROWS, near.shape[1])], [], near, doms[turns.index(0)])
    onward = [(i, (i + (2 if i % 2 == 0 else -2)) % count) for i in range(count)]
    return doms + [near, lax.ppermute(kept, "sub", onward)]


def on_device(
    modal_state,
    stiffness,
    jacobians,
    flux_solvers,
    projector,
    rotations,
    yield_stress,
    cluster,
    orient,
    neighbour_slot,
    send_map,
):
    basis, quants, lanes = modal_state.shape
    inputs = [
        send_map.reshape(1, -1),
        jnp.transpose(projector, (1, 0, 2)),
        stiffness,
        jnp.transpose(modal_state, (1, 0, 2)),
        jnp.transpose(jacobians, (1, 2, 0, 3)),
        jnp.transpose(flux_solvers, (0, 2, 3, 1, 4)),
        rotations,
        neighbour_slot,
        orient,
        cluster.reshape(1, lanes),
        yield_stress.reshape(1, lanes),
    ]
    inputs = [pltpu.with_memory_space_constraint(item, pltpu.HBM) for item in inputs]
    held = [jax.ShapeDtypeStruct(item.shape, item.dtype) for item in inputs]

    field = (quants, basis, lanes)
    table = (quants * ROWS, 4 * lanes)
    dom_message = (DOM_GROUPS[0][1] * ROWS, lanes)
    messages = [dom_message, dom_message, (2 * SUB_ROWS, lanes)]
    choice = jax.ShapeDtypeStruct((4 * lanes, 4 * lanes), BF16)
    flat = quants * lanes
    fold = (3 * basis, 3 * fold_step(basis))
    stiffened = pltpu.VMEM((3 * basis, flat), F32)
    two_stiffened = pltpu.VMEM((2, 3 * basis, flat), F32)

    outs = run(
        first_kernel,
        held + [field, field, table, (4 * ROWS, 128), fold, choice] + messages,
        [two_stiffened, pltpu.SemaphoreType.DMA((INPUTS,))],
        *inputs, space=pl.ANY,
    )
    _, _, stiff, state, jac, flux, turns, slot, orient, cluster, limit = outs[:INPUTS]
    first, second, table_one, padded, stiff_fold, sending, *sends = outs[INPUTS:]
    arrived = exchange(sends, FIRST_TURNS)
    part_one, local_one, lifting, turned_fold, received = run(
        second_kernel, [field, table, (basis, 3 * 4 * ROWS), fold, choice], [stiffened],
        state, first, table_one, jac, stiff, padded, turns, flux, slot,
    )
    middle, integral, picked_one, table_two, *sends = run(
        third_kernel, [field, field, table, table] + messages, [two_stiffened],
        state, first, second, part_one, local_one, *arrived,
        jac, stiff_fold, padded, flux, orient, cluster, lifting, received, sending,
    )
    arrived = exchange(sends, SECOND_TURNS)
    part_two, local_two = run(
        fourth_kernel, [field, table], [stiffened, pltpu.VMEM(table, F32)],
        middle, integral, table_one, table_two, picked_one, jac, turned_fold, padded, flux,
        slot, cluster,
    )
    updated, = run(
        fifth_kernel, [field], [pltpu.VMEM(table, F32)],
        part_two, local_two, *arrived, flux, orient, lifting, received, limit,
    )
    return jnp.transpose(updated, (1, 0, 2))


def solution(mesh):
    placed = (
        P(None, None, ("dom", "sub")),
        P(),
        P(None, None, None, ("dom", "sub")),
        P(None, None, None, None, ("dom", "sub")),
        P(),
        P(),
        P(("dom", "sub")),
        P(("dom", "sub")),
        P(None, ("dom", "sub")),
        P(None, ("dom", "sub")),
        P(("dom", "sub")),
    )
    return jax.shard_map(
        on_device,
        mesh=mesh,
        in_specs=placed,
        out_specs=P(None, None, ("dom", "sub")),
        check_vma=False,
    )
```

profile of v0, /device:TPU:0, one launch (start us, length us, event | category | flops | bytes accessed | tf_op | source)
XLA Modules:
  0.0 31.5 jit_solution(5099624711524706370)
XLA Ops:
  0.0 6.1 %first_kernel.1 = (s32[1,192]{1,0:T(1,128)}, f32[21,4,56]{2,1,0:T(4,128)}, f32[3,56,56]{2,1,0:T(8,128)S(1)}, f32[9,56,128]{2,1,0:T(8,128)S(1)}, f32[9,9,3,128]{3...) custom-call(s32[1,192]{1,0:T(1,128)} %bitcast.12, ...), custom_call_target="tpu_custom_call" | custom-call | tf_op jit(solution)/shard_map/first_kernel/pallas_call | solution.py:458
  6.1 3.0 %collective-permute-start.2 = (f32[144,128]{1,0:T(8,128)S(1)}, f32[144,128]{1,0:T(8,128)S(1)}, u32[]{:S(2)}, u32[]{:S(2)}) collective-permute-start(f32[144,128]{1,0:T(8,128)S(1)} %get-tuple-element.51), channel_id=1, source_target_pairs={{0,1},{2,3},{1,0},{3,2},{4,5},{6,7},{5,4},{7,6},{8,9},{10,11},{9,8... | collective-permute-start | bytes 221192 | tf_op jit(solution)/shard_map/ppermute | solution.py:479
  9.1 0.0 collective-permute-start.1
  9.1 0.7 %collective-permute-start = (f32[120,128]{1,0:T(8,128)S(1)}, f32[120,128]{1,0:T(8,128)S(1)}, u32[]{:S(2)}, u32[]{:S(2)}) collective-permute-start(f32[120,128]{1,0:T(8,128)S(1)} %get-tuple-element.49), channel_id=1, source_target_pairs={{4,8},{12,16},{20,24},{8,4},{16,12},{24,20},{5,9},{13,17},{21,25},... | collective-permute-start | bytes 184328 | tf_op jit(solution)/shard_map/ppermute | solution.py:479
  9.8 0.6 %collective-permute-done.1.dom.dom_b = f32[120,128]{1,0:T(8,128)S(1)} collective-permute-done((f32[120,128]{1,0:T(8,128)S(1)}, f32[120,128]{1,0:T(8,128)S(1)}, u32[]{:S(2)}, u32[]{:S(2)}) %collective-permute-start.1) | collective-permute-done | bytes 61472 | tf_op jit(solution)/shard_map/ppermute | solution.py:479
  10.4 1.1 %collective-permute-done.2.near.sub_near = f32[144,128]{1,0:T(8,128)S(1)} collective-permute-done((f32[144,128]{1,0:T(8,128)S(1)}, f32[144,128]{1,0:T(8,128)S(1)}, u32[]{:S(2)}, u32[]{:S(2)}) %collective-permute-start.2) | collective-permute-done | bytes 73760 | tf_op jit(solution)/shard_map/ppermute | solution.py:479
  11.4 2.0 %collective-permute-start.3 = (f32[72,128]{1,0:T(8,128)S(1)}, f32[72,128]{1,0:T(8,128)S(1)}, u32[]{:S(2)}, u32[]{:S(2)}) collective-permute-start(f32[72,128]{1,0:T(8,128)S(1)} %hand_on.2), channel_id=1, source_target_pairs={{0,2},{1,3},{2,0},{3,1},{4,6},{5,7},{6,4},{7,5},{8,10},{9,11},{10,... | collective-permute-start | bytes 110600 | tf_op jit(solution)/shard_map/ppermute | solution.py:488
  13.5 2.2 %second_kernel.1 = (f32[9,56,128]{2,1,0:T(8,128)S(1)}, f32[216,512]{1,0:T(8,128)S(1)}, f32[56,288]{1,0:T(8,128)S(1)}, f32[168,192]{1,0:T(8,128)S(1)}, bf16[512,512]{1,0:T(8,128)(2,1)S(1)}) custom-call(f32[9,56,128]{2,1,0:T(8,128)S(1)} %get-tuple-element.37.state, f32[9,56,128]{2,1,0:T(8,128)S(1)} %get-tuple-element.38.first, ...), custom_call_target="tpu_custom_call" | custom-call | tf_op jit(solution)/shard_map/second_kernel/pallas_call | solution.py:458
  15.7 0.0 collective-permute-done.dom_a
  15.7 0.0 collective-permute-done.3.sub_far
  15.7 5.1 %third_kernel.1 = (f32[9,56,128]{2,1,0:T(8,128)S(1)}, f32[9,56,128]{2,1,0:T(8,128)S(1)}, f32[216,512]{1,0:T(8,128)S(1)}, f32[216,512]{1,0:T(8,128)S(1)}, f32[120...) custom-call(f32[9,56,128]{2,1,0:T(8,128)S(1)} %get-tuple-element.37.state, ...), custom_call_target="tpu_custom_call" | custom-call | tf_op jit(solution)/shard_map/third_kernel/pallas_call | solution.py:458
  20.8 1.8 %collective-permute-start.6 = (f32[144,128]{1,0:T(8,128)S(1)}, f32[144,128]{1,0:T(8,128)S(1)}, u32[]{:S(2)}, u32[]{:S(2)}) collective-permute-start(f32[144,128]{1,0:T(8,128)S(1)} %get-tuple-element.67), channel_id=1, source_target_pairs={{0,1},{2,3},{1,0},{3,2},{4,5},{6,7},{5,4},{7,6},{8,9},{10,11},{9,8... | collective-permute-start | bytes 221192 | tf_op jit(solution)/shard_map/ppermute | solution.py:479
  22.6 0.0 collective-permute-start.5
  22.6 0.7 %collective-permute-start.4 = (f32[120,128]{1,0:T(8,128)S(1)}, f32[120,128]{1,0:T(8,128)S(1)}, u32[]{:S(2)}, u32[]{:S(2)}) collective-permute-start(f32[120,128]{1,0:T(8,128)S(1)} %get-tuple-element.65), channel_id=1, source_target_pairs={{4,8},{12,16},{20,24},{8,4},{16,12},{24,20},{5,9},{13,17},{21,25},... | collective-permute-start | bytes 184328 | tf_op jit(solution)/shard_map/ppermute | solution.py:479
  23.2 0.6 %collective-permute-done.5.dom.dom_b = f32[120,128]{1,0:T(8,128)S(1)} collective-permute-done((f32[120,128]{1,0:T(8,128)S(1)}, f32[120,128]{1,0:T(8,128)S(1)}, u32[]{:S(2)}, u32[]{:S(2)}) %collective-permute-start.5) | collective-permute-done | bytes 61472 | tf_op jit(solution)/shard_map/ppermute | solution.py:479
  23.8 1.7 %collective-permute-done.6.near.sub_near = f32[144,128]{1,0:T(8,128)S(1)} collective-permute-done((f32[144,128]{1,0:T(8,128)S(1)}, f32[144,128]{1,0:T(8,128)S(1)}, u32[]{:S(2)}, u32[]{:S(2)}) %collective-permute-start.6) | collective-permute-done | bytes 73760 | tf_op jit(solution)/shard_map/ppermute | solution.py:479
  25.6 1.6 %collective-permute-start.7 = (f32[72,128]{1,0:T(8,128)S(1)}, f32[72,128]{1,0:T(8,128)S(1)}, u32[]{:S(2)}, u32[]{:S(2)}) collective-permute-start(f32[72,128]{1,0:T(8,128)S(1)} %hand_on.3), channel_id=1, source_target_pairs={{0,2},{1,3},{2,0},{3,1},{4,6},{5,7},{6,4},{7,5},{8,10},{9,11},{10,... | collective-permute-start | bytes 110600 | tf_op jit(solution)/shard_map/ppermute | solution.py:488
  27.2 1.5 %fourth_kernel.1 = (f32[9,56,128]{2,1,0:T(8,128)S(1)}, f32[216,512]{1,0:T(8,128)S(1)}) custom-call(f32[9,56,128]{2,1,0:T(8,128)S(1)} %get-tuple-element.58.middle, f32[9,56,128]{2,1,0:T(8,128)S(1)} %get-tuple-element.59.integral, f32[216,512]{1,0:T(8,128)S(1)} %get-tuple-element.40.table.table_one, f32[216,512]{1,0:T(8,128)S(1)} %get-tuple-element.60.table_two, ...), custom_call_target="tpu_custom_call" | custom-call | tf_op jit(solution)/shard_map/fourth_kernel/pallas_call | solution.py:458
  28.7 0.0 collective-permute-done.4.dom_a
  28.7 0.9 %collective-permute-done.7.sub_far = f32[72,128]{1,0:T(8,128)S(1)} collective-permute-done((f32[72,128]{1,0:T(8,128)S(1)}, f32[72,128]{1,0:T(8,128)S(1)}, u32[]{:S(2)}, u32[]{:S(2)}) %collective-permute-start.7) | collective-permute-done | bytes 36896 | tf_op jit(solution)/shard_map/ppermute | solution.py:488
  29.7 1.8 %fifth_kernel.1 = f32[9,56,128]{2,1,0:T(8,128)} custom-call(f32[9,56,128]{2,1,0:T(8,128)S(1)} %get-tuple-element.63.part, f32[216,512]{1,0:T(8,128)S(1)} %get-tuple-element.64.picked_local, f32[120,128]{1,0:T(8,128)S(1)} %collective-permute-done.4.dom_a, f32[120,128]{1,0:T(8,128)S(1)} %collective-permute-done.5.dom.dom_b, ...), custom_call_target="tpu_custom_call" | custom-call | tf_op jit(solution)/shard_map/fifth_kernel/pallas_call | solution.py:458
  (2 shorter events, 0.0 us)
Async XLA Ops:
  6.1 5.3 %collective-permute-start.2 = (f32[144,128]{1,0:T(8,128)S(1)}, f32[144,128]{1,0:T(8,128)S(1)}, u32[]{:S(2)}, u32[]{:S(2)}) collective-permute-start(f32[144,128]{1,0:T(8,128)S(1)} %get-tuple-element.51), channel_id=1, source_target_pairs={{0,1},{2,3},{1,0},{3,2},{4,5},{6,7},{5,4},{7,6},{8,9},{10,11},{9,8... | collective-permute-start | bytes 221192 | tf_op jit(solution)/shard_map/ppermute | solution.py:479
  9.1 1.2 %collective-permute-start.1 = (f32[120,128]{1,0:T(8,128)S(1)}, f32[120,128]{1,0:T(8,128)S(1)}, u32[]{:S(2)}, u32[]{:S(2)}) collective-permute-start(f32[120,128]{1,0:T(8,128)S(1)} %get-tuple-element.50), channel_id=1, source_target_pairs={{0,4},{8,12},{16,20},{24,28},{4,0},{12,8},{20,16},{28,24},{1,5},{9... | collective-permute-start | bytes 184328 | tf_op jit(solution)/shard_map/ppermute | solution.py:479
  9.1 6.6 %collective-permute-start = (f32[120,128]{1,0:T(8,128)S(1)}, f32[120,128]{1,0:T(8,128)S(1)}, u32[]{:S(2)}, u32[]{:S(2)}) collective-permute-start(f32[120,128]{1,0:T(8,128)S(1)} %get-tuple-element.49), channel_id=1, source_target_pairs={{4,8},{12,16},{20,24},{8,4},{16,12},{24,20},{5,9},{13,17},{21,25},... | collective-permute-start | bytes 184328 | tf_op jit(solution)/shard_map/ppermute | solution.py:479
  11.4 4.2 %collective-permute-start.3 = (f32[72,128]{1,0:T(8,128)S(1)}, f32[72,128]{1,0:T(8,128)S(1)}, u32[]{:S(2)}, u32[]{:S(2)}) collective-permute-start(f32[72,128]{1,0:T(8,128)S(1)} %hand_on.2), channel_id=1, source_target_pairs={{0,2},{1,3},{2,0},{3,1},{4,6},{5,7},{6,4},{7,5},{8,10},{9,11},{10,... | collective-permute-start | bytes 110600 | tf_op jit(solution)/shard_map/ppermute | solution.py:488
  20.8 4.8 %collective-permute-start.6 = (f32[144,128]{1,0:T(8,128)S(1)}, f32[144,128]{1,0:T(8,128)S(1)}, u32[]{:S(2)}, u32[]{:S(2)}) collective-permute-start(f32[144,128]{1,0:T(8,128)S(1)} %get-tuple-element.67), channel_id=1, source_target_pairs={{0,1},{2,3},{1,0},{3,2},{4,5},{6,7},{5,4},{7,6},{8,9},{10,11},{9,8... | collective-permute-start | bytes 221192 | tf_op jit(solution)/shard_map/ppermute | solution.py:479
  22.6 1.2 %collective-permute-start.5 = (f32[120,128]{1,0:T(8,128)S(1)}, f32[120,128]{1,0:T(8,128)S(1)}, u32[]{:S(2)}, u32[]{:S(2)}) collective-permute-start(f32[120,128]{1,0:T(8,128)S(1)} %get-tuple-element.66), channel_id=1, source_target_pairs={{0,4},{8,12},{16,20},{24,28},{4,0},{12,8},{20,16},{28,24},{1,5},{9... | collective-permute-start | bytes 184328 | tf_op jit(solution)/shard_map/ppermute | solution.py:479
  22.6 6.1 %collective-permute-start.4 = (f32[120,128]{1,0:T(8,128)S(1)}, f32[120,128]{1,0:T(8,128)S(1)}, u32[]{:S(2)}, u32[]{:S(2)}) collective-permute-start(f32[120,128]{1,0:T(8,128)S(1)} %get-tuple-element.65), channel_id=1, source_target_pairs={{4,8},{12,16},{20,24},{8,4},{16,12},{24,20},{5,9},{13,17},{21,25},... | collective-permute-start | bytes 184328 | tf_op jit(solution)/shard_map/ppermute | solution.py:479
  25.6 4.1 %collective-permute-start.7 = (f32[72,128]{1,0:T(8,128)S(1)}, f32[72,128]{1,0:T(8,128)S(1)}, u32[]{:S(2)}, u32[]{:S(2)}) collective-permute-start(f32[72,128]{1,0:T(8,128)S(1)} %hand_on.3), channel_id=1, source_target_pairs={{0,2},{1,3},{2,0},{3,1},{4,6},{5,7},{6,4},{7,5},{8,10},{9,11},{10,... | collective-permute-start | bytes 110600 | tf_op jit(solution)/shard_map/ppermute | solution.py:488
where the time goes:
time: 31.6 us; the launch traced here: 31.5 us
  Pallas kernels  16.6 us (53%)
  starting transfers between devices  9.81 us (31%)
  waiting for transfers between devices  4.93 us (16%)
    pallas_call x7, Pallas kernels, run(): pl.pallas_call(body, out_shape=[out if isinstance(out, jax.ShapeDtypeStru...  16.6 us
    ppermute x6, starting transfers between devices, swap(): lax.ppermute(value, axis, [(i, i + 1) for i in lower] + [(i + 1, i) for i...  6.12 us
    ppermute x6, waiting for transfers between devices, swap(): lax.ppermute(value, axis, [(i, i + 1) for i in lower] + [(i + 1, i) for i...  4 us
    ppermute x2, starting transfers between devices, exchange(): return doms + [near, lax.ppermute(kept, 'sub', onward)]  3.7 us
    ppermute x2, waiting for transfers between devices, exchange(): return doms + [near, lax.ppermute(kept, 'sub', onward)]  0.93 us
  transfers between devices with their start and end apart: 8, of which 5 were waited for; matrix products, arithmetic and copies ran while one was open for 0% of the time, Pallas kernels for 12%

commit v1 on v0

--- a/solution.py
+++ b/solution.py
@@ -24,7 +24,7 @@
 SUB_ROWS = SUB_GROUPS[0][1] * ROWS
 
 FIRST_TURNS = (1, 0)
-SECOND_TURNS = (1, 0)
+SECOND_TURNS = (0, 1)
 
 
 INPUTS = 11
@@ -53,6 +53,17 @@
     if modulus is not None:
         number = lax.rem(number, modulus)
     return jnp.where(number + first == index_row, 1.0, 0.0).astype(BF16)
+
+
+def stack_rows(value):
+    high = value.astype(BF16).astype(F32)
+    return jnp.concatenate([high, value - high], axis=0).astype(BF16)
+
+
+def gather(table, chosen):
+    rows = table.shape[0]
+    both = dot(stack_rows(table), chosen)
+    return both[0:rows] + both[rows:2 * rows]
 
 
 def fold_step(basis):
@@ -175,8 +186,7 @@
 
 
 def pick_sends(table, chosen, outs, turns, lanes):
-    upper, lower = halves(table[...])
-    sent = dot(upper, chosen) + dot(lower, chosen)
+    sent = gather(table[...], chosen)
     for k, groups in enumerate(PACKING):
         out = outs[turns.index(k)] if k < 2 else outs[2]
         row = SUB_ROWS if k == 3 else 0
@@ -208,8 +218,7 @@
 
 def pick_local(table, slot, faces):
     chosen = jnp.concatenate([one_hot(slot[f:f + 1], 0, faces) for f in range(4)], axis=1)
-    upper, lower = halves(table)
-    return dot(upper, chosen) + dot(lower, chosen)
+    return gather(table, chosen)
 
 
 def received_choice(slot, faces, lanes):
@@ -245,12 +254,20 @@
         [spread_received(item, groups, lanes) for item, groups in zip(pieces, PACKING)],
         axis=1,
     )
-    upper, lower = halves(spread)
-    return dot(upper, chosen) + dot(lower, chosen)
-
-
-def lift(upper, lower, high, low):
-    return dot(upper, high) + dot(lower, high) + dot(upper, low)
+    return gather(spread, chosen)
+
+
+def lift_weights(lifting):
+    basis, depth = lifting.shape
+    rest = jnp.zeros((fold_step(basis) - basis, depth), F32)
+    high, low = halves(jnp.concatenate([lifting, rest], axis=0))
+    return jnp.concatenate([high, low], axis=0)
+
+
+def lift(weights, high, low, basis):
+    step = fold_step(basis)
+    both = dot(weights, high)
+    return both[0:basis] + both[step:step + basis] + dot(weights[0:step], low)[0:basis]
 
 
 def local_update(
@@ -260,11 +277,11 @@
     for start in range(0, quants, GROUP):
         values = [integral(q) for q in range(start, start + GROUP)]
         stiffen(turned_fold, values, stiffened, start, lanes)
-    upper, lower = halves(lifting)
+    weights = lift_weights(lifting)
     for start in range(0, quants, GROUP):
         solved = mix_faces(table, flux, 0, start, quants, lanes)
         high, low = halves(jnp.concatenate(solved, axis=1))
-        own = lift(upper, lower, high, low)
+        own = lift(weights, high, low, basis)
         for i in range(GROUP):
             part[start + i] = base(start + i) - own[:, i * lanes:(i + 1) * lanes]
 
@@ -276,7 +293,7 @@
 
 
 def near_lift(picked, flux, orient, lifting, quants, lanes, take):
-    upper, lower = halves(lifting)
+    weights = lift_weights(lifting)
     masks = [
         jnp.concatenate(
             [
@@ -294,7 +311,8 @@
             highs.append(jnp.concatenate([high * mask for mask in masks], axis=0))
             lows.append(jnp.concatenate([low * mask for mask in masks], axis=0))
         near = lift(
-            upper, lower, jnp.concatenate(highs, axis=1), jnp.concatenate(lows, axis=1)
+            weights, jnp.concatenate(highs, axis=1), jnp.concatenate(lows, axis=1),
+            lifting.shape[0],
         )
         for i in range(GROUP):
             take(start + i, near[:, i * lanes:(i + 1) * lanes])
@@ -483,7 +501,7 @@
     count = lax.axis_size("sub")
     near = swap(sends[2], "sub", 0)
     doms = [swap(value, "dom", first) for value, first in zip(sends, turns)]
-    kept, = run(hand_on, [(SUB_ROWS, near.shape[1])], [], near, doms[turns.index(0)])
+    kept, = run(hand_on, [(SUB_ROWS, near.shape[1])], [], near, doms[0])
     onward = [(i, (i + (2 if i % 2 == 0 else -2)) % count) for i in range(count)]
     return doms + [near, lax.ppermute(kept, "sub", onward)]
 

time: 31.6 us -> 32.7 us (1.035)
  starting transfers between devices: 9.81 us -> 12.1 us
  waiting for transfers between devices: 4.93 us -> 3.83 us
    ppermute x6, starting transfers between devices: 6.12 us -> 8.93 us  [swap(): lax.ppermute(value, axis, [(i, i + 1) for i in lower] + [(i + 1, i) for i...]
    ppermute x6, waiting for transfers between devices: 4 us -> 2.6 us  [swap(): lax.ppermute(value, axis, [(i, i + 1) for i in lower] + [(i + 1, i) for i...]
    ppermute x2, starting transfers between devices: 3.7 us -> 3.15 us  [exchange(): return doms + [near, lax.ppermute(kept, 'sub', onward)]]
  transfers between devices with their start and end apart: 8 -> 8, of which waited for: 5 -> 4; matrix products, arithmetic and copies ran while one was open for 0% -> 0% of each run, Pallas kernels for 12% -> 11%
where the time goes in v1:
time: 32.7 us; the launch traced here: 32.5 us
  Pallas kernels  16.5 us (50%)
  starting transfers between devices  12.1 us (37%)
  waiting for transfers between devices  3.83 us (12%)
    pallas_call x7, Pallas kernels, run(): pl.pallas_call(body, out_shape=[out if isinstance(out, jax.ShapeDtypeStru...  16.5 us
    ppermute x6, starting transfers between devices, swap(): lax.ppermute(value, axis, [(i, i + 1) for i in lower] + [(i + 1, i) for i...  8.93 us
    ppermute x2, starting transfers between devices, exchange(): return doms + [near, lax.ppermute(kept, 'sub', onward)]  3.15 us
    ppermute x6, waiting for transfers between devices, swap(): lax.ppermute(value, axis, [(i, i + 1) for i in lower] + [(i + 1, i) for i...  2.6 us
    ppermute x2, waiting for transfers between devices, exchange(): return doms + [near, lax.ppermute(kept, 'sub', onward)]  1.23 us
  transfers between devices with their start and end apart: 8, of which 4 were waited for; matrix products, arithmetic and copies ran while one was open for 0% of the time, Pallas kernels for 11%

profile of v1, /device:TPU:0, one launch (start us, length us, event | category | flops | bytes accessed | tf_op | source)
XLA Modules:
  0.0 32.5 jit_solution(13426491046421948393)
XLA Ops:
  0.0 6.1 %first_kernel.1 = (s32[1,192]{1,0:T(1,128)}, f32[21,4,56]{2,1,0:T(4,128)}, f32[3,56,56]{2,1,0:T(8,128)S(1)}, f32[9,56,128]{2,1,0:T(8,128)S(1)}, f32[9,9,3,128]{3...) custom-call(s32[1,192]{1,0:T(1,128)} %bitcast.12, ...), custom_call_target="tpu_custom_call" | custom-call | tf_op jit(solution)/shard_map/first_kernel/pallas_call | solution.py:476
  6.1 3.0 %collective-permute-start.2 = (f32[144,128]{1,0:T(8,128)S(1)}, f32[144,128]{1,0:T(8,128)S(1)}, u32[]{:S(2)}, u32[]{:S(2)}) collective-permute-start(f32[144,128]{1,0:T(8,128)S(1)} %get-tuple-element.51), channel_id=1, source_target_pairs={{0,1},{2,3},{1,0},{3,2},{4,5},{6,7},{5,4},{7,6},{8,9},{10,11},{9,8... | collective-permute-start | bytes 221192 | tf_op jit(solution)/shard_map/ppermute | solution.py:497
  9.1 0.7 %collective-permute-start = (f32[120,128]{1,0:T(8,128)S(1)}, f32[120,128]{1,0:T(8,128)S(1)}, u32[]{:S(2)}, u32[]{:S(2)}) collective-permute-start(f32[120,128]{1,0:T(8,128)S(1)} %get-tuple-element.49), channel_id=1, source_target_pairs={{4,8},{12,16},{20,24},{8,4},{16,12},{24,20},{5,9},{13,17},{21,25},... | collective-permute-start | bytes 184328 | tf_op jit(solution)/shard_map/ppermute | solution.py:497
  9.8 3.0 %collective-permute-start.1 = (f32[120,128]{1,0:T(8,128)S(1)}, f32[120,128]{1,0:T(8,128)S(1)}, u32[]{:S(2)}, u32[]{:S(2)}) collective-permute-start(f32[120,128]{1,0:T(8,128)S(1)} %get-tuple-element.50), channel_id=1, source_target_pairs={{0,4},{8,12},{16,20},{24,28},{4,0},{12,8},{20,16},{28,24},{1,5},{9... | collective-permute-start | bytes 184328 | tf_op jit(solution)/shard_map/ppermute | solution.py:497
  12.8 0.0 collective-permute-done.dom.dom_a
  12.8 0.0 collective-permute-done.2.near.sub_near
  12.8 1.6 %collective-permute-start.3 = (f32[72,128]{1,0:T(8,128)S(1)}, f32[72,128]{1,0:T(8,128)S(1)}, u32[]{:S(2)}, u32[]{:S(2)}) collective-permute-start(f32[72,128]{1,0:T(8,128)S(1)} %hand_on.2), channel_id=1, source_target_pairs={{0,2},{1,3},{2,0},{3,1},{4,6},{5,7},{6,4},{7,5},{8,10},{9,11},{10,... | collective-permute-start | bytes 110600 | tf_op jit(solution)/shard_map/ppermute | solution.py:506
  14.4 2.2 %second_kernel.1 = (f32[9,56,128]{2,1,0:T(8,128)S(1)}, f32[216,512]{1,0:T(8,128)S(1)}, f32[56,288]{1,0:T(8,128)S(1)}, f32[168,192]{1,0:T(8,128)S(1)}, bf16[512,512]{1,0:T(8,128)(2,1)S(1)}) custom-call(f32[9,56,128]{2,1,0:T(8,128)S(1)} %get-tuple-element.37.state, f32[9,56,128]{2,1,0:T(8,128)S(1)} %get-tuple-element.38.first, ...), custom_call_target="tpu_custom_call" | custom-call | tf_op jit(solution)/shard_map/second_kernel/pallas_call | solution.py:476
  16.5 0.0 collective-permute-done.1.dom_b
  16.5 0.2 collective-permute-done.3.sub_far
  16.8 5.0 %third_kernel.1 = (f32[9,56,128]{2,1,0:T(8,128)S(1)}, f32[9,56,128]{2,1,0:T(8,128)S(1)}, f32[216,512]{1,0:T(8,128)S(1)}, f32[216,512]{1,0:T(8,128)S(1)}, f32[120...) custom-call(f32[9,56,128]{2,1,0:T(8,128)S(1)} %get-tuple-element.37.state, ...), custom_call_target="tpu_custom_call" | custom-call | tf_op jit(solution)/shard_map/third_kernel/pallas_call | solution.py:476
  21.8 0.7 %collective-permute-start.6 = (f32[144,128]{1,0:T(8,128)S(1)}, f32[144,128]{1,0:T(8,128)S(1)}, u32[]{:S(2)}, u32[]{:S(2)}) collective-permute-start(f32[144,128]{1,0:T(8,128)S(1)} %get-tuple-element.67), channel_id=1, source_target_pairs={{0,1},{2,3},{1,0},{3,2},{4,5},{6,7},{5,4},{7,6},{8,9},{10,11},{9,8... | collective-permute-start | bytes 221192 | tf_op jit(solution)/shard_map/ppermute | solution.py:497
  22.5 0.9 %collective-permute-start.4 = (f32[120,128]{1,0:T(8,128)S(1)}, f32[120,128]{1,0:T(8,128)S(1)}, u32[]{:S(2)}, u32[]{:S(2)}) collective-permute-start(f32[120,128]{1,0:T(8,128)S(1)} %get-tuple-element.65), channel_id=1, source_target_pairs={{0,4},{8,12},{16,20},{24,28},{4,0},{12,8},{20,16},{28,24},{1,5},{9... | collective-permute-start | bytes 184328 | tf_op jit(solution)/shard_map/ppermute | solution.py:497
  23.4 0.7 %collective-permute-start.5 = (f32[120,128]{1,0:T(8,128)S(1)}, f32[120,128]{1,0:T(8,128)S(1)}, u32[]{:S(2)}, u32[]{:S(2)}) collective-permute-start(f32[120,128]{1,0:T(8,128)S(1)} %get-tuple-element.66), channel_id=1, source_target_pairs={{4,8},{12,16},{20,24},{8,4},{16,12},{24,20},{5,9},{13,17},{21,25},... | collective-permute-start | bytes 184328 | tf_op jit(solution)/shard_map/ppermute | solution.py:497
  24.1 0.2 collective-permute-done.4.dom.dom_a
  24.3 2.4 %collective-permute-done.6.near.sub_near = f32[144,128]{1,0:T(8,128)S(1)} collective-permute-done((f32[144,128]{1,0:T(8,128)S(1)}, f32[144,128]{1,0:T(8,128)S(1)}, u32[]{:S(2)}, u32[]{:S(2)}) %collective-permute-start.6) | collective-permute-done | bytes 73760 | tf_op jit(solution)/shard_map/ppermute | solution.py:497
  26.7 1.6 %collective-permute-start.7 = (f32[72,128]{1,0:T(8,128)S(1)}, f32[72,128]{1,0:T(8,128)S(1)}, u32[]{:S(2)}, u32[]{:S(2)}) collective-permute-start(f32[72,128]{1,0:T(8,128)S(1)} %hand_on.3), channel_id=1, source_target_pairs={{0,2},{1,3},{2,0},{3,1},{4,6},{5,7},{6,4},{7,5},{8,10},{9,11},{10,... | collective-permute-start | bytes 110600 | tf_op jit(solution)/shard_map/ppermute | solution.py:506
  28.3 1.5 %fourth_kernel.1 = (f32[9,56,128]{2,1,0:T(8,128)S(1)}, f32[216,512]{1,0:T(8,128)S(1)}) custom-call(f32[9,56,128]{2,1,0:T(8,128)S(1)} %get-tuple-element.58.middle, f32[9,56,128]{2,1,0:T(8,128)S(1)} %get-tuple-element.59.integral, f32[216,512]{1,0:T(8,128)S(1)} %get-tuple-element.40.table.table_one, f32[216,512]{1,0:T(8,128)S(1)} %get-tuple-element.60.table_two, ...), custom_call_target="tpu_custom_call" | custom-call | tf_op jit(solution)/shard_map/fourth_kernel/pallas_call | solution.py:476
  29.7 0.0 collective-permute-done.5.dom_b
  29.8 1.0 %collective-permute-done.7.sub_far = f32[72,128]{1,0:T(8,128)S(1)} collective-permute-done((f32[72,128]{1,0:T(8,128)S(1)}, f32[72,128]{1,0:T(8,128)S(1)}, u32[]{:S(2)}, u32[]{:S(2)}) %collective-permute-start.7) | collective-permute-done | bytes 36896 | tf_op jit(solution)/shard_map/ppermute | solution.py:506
  30.7 1.7 %fifth_kernel.1 = f32[9,56,128]{2,1,0:T(8,128)} custom-call(f32[9,56,128]{2,1,0:T(8,128)S(1)} %get-tuple-element.63.part, f32[216,512]{1,0:T(8,128)S(1)} %get-tuple-element.64.picked_local, f32[120,128]{1,0:T(8,128)S(1)} %collective-permute-done.4.dom.dom_a, f32[120,128]{1,0:T(8,128)S(1)} %collective-permute-done.5.dom_b, ...), custom_call_target="tpu_custom_call" | custom-call | tf_op jit(solution)/shard_map/fifth_kernel/pallas_call | solution.py:476
  (2 shorter events, 0.0 us)
Async XLA Ops:
  6.1 6.7 %collective-permute-start.2 = (f32[144,128]{1,0:T(8,128)S(1)}, f32[144,128]{1,0:T(8,128)S(1)}, u32[]{:S(2)}, u32[]{:S(2)}) collective-permute-start(f32[144,128]{1,0:T(8,128)S(1)} %get-tuple-element.51), channel_id=1, source_target_pairs={{0,1},{2,3},{1,0},{3,2},{4,5},{6,7},{5,4},{7,6},{8,9},{10,11},{9,8... | collective-permute-start | bytes 221192 | tf_op jit(solution)/shard_map/ppermute | solution.py:497
  9.1 3.7 %collective-permute-start = (f32[120,128]{1,0:T(8,128)S(1)}, f32[120,128]{1,0:T(8,128)S(1)}, u32[]{:S(2)}, u32[]{:S(2)}) collective-permute-start(f32[120,128]{1,0:T(8,128)S(1)} %get-tuple-element.49), channel_id=1, source_target_pairs={{4,8},{12,16},{20,24},{8,4},{16,12},{24,20},{5,9},{13,17},{21,25},... | collective-permute-start | bytes 184328 | tf_op jit(solution)/shard_map/ppermute | solution.py:497
  9.8 6.8 %collective-permute-start.1 = (f32[120,128]{1,0:T(8,128)S(1)}, f32[120,128]{1,0:T(8,128)S(1)}, u32[]{:S(2)}, u32[]{:S(2)}) collective-permute-start(f32[120,128]{1,0:T(8,128)S(1)} %get-tuple-element.50), channel_id=1, source_target_pairs={{0,4},{8,12},{16,20},{24,28},{4,0},{12,8},{20,16},{28,24},{1,5},{9... | collective-permute-start | bytes 184328 | tf_op jit(solution)/shard_map/ppermute | solution.py:497
  12.8 4.0 %collective-permute-start.3 = (f32[72,128]{1,0:T(8,128)S(1)}, f32[72,128]{1,0:T(8,128)S(1)}, u32[]{:S(2)}, u32[]{:S(2)}) collective-permute-start(f32[72,128]{1,0:T(8,128)S(1)} %hand_on.2), channel_id=1, source_target_pairs={{0,2},{1,3},{2,0},{3,1},{4,6},{5,7},{6,4},{7,5},{8,10},{9,11},{10,... | collective-permute-start | bytes 110600 | tf_op jit(solution)/shard_map/ppermute | solution.py:506
  21.8 4.9 %collective-permute-start.6 = (f32[144,128]{1,0:T(8,128)S(1)}, f32[144,128]{1,0:T(8,128)S(1)}, u32[]{:S(2)}, u32[]{:S(2)}) collective-permute-start(f32[144,128]{1,0:T(8,128)S(1)} %get-tuple-element.67), channel_id=1, source_target_pairs={{0,1},{2,3},{1,0},{3,2},{4,5},{6,7},{5,4},{7,6},{8,9},{10,11},{9,8... | collective-permute-start | bytes 221192 | tf_op jit(solution)/shard_map/ppermute | solution.py:497
  22.5 1.8 %collective-permute-start.4 = (f32[120,128]{1,0:T(8,128)S(1)}, f32[120,128]{1,0:T(8,128)S(1)}, u32[]{:S(2)}, u32[]{:S(2)}) collective-permute-start(f32[120,128]{1,0:T(8,128)S(1)} %get-tuple-element.65), channel_id=1, source_target_pairs={{0,4},{8,12},{16,20},{24,28},{4,0},{12,8},{20,16},{28,24},{1,5},{9... | collective-permute-start | bytes 184328 | tf_op jit(solution)/shard_map/ppermute | solution.py:497
  23.4 6.3 %collective-permute-start.5 = (f32[120,128]{1,0:T(8,128)S(1)}, f32[120,128]{1,0:T(8,128)S(1)}, u32[]{:S(2)}, u32[]{:S(2)}) collective-permute-start(f32[120,128]{1,0:T(8,128)S(1)} %get-tuple-element.66), channel_id=1, source_target_pairs={{4,8},{12,16},{20,24},{8,4},{16,12},{24,20},{5,9},{13,17},{21,25},... | collective-permute-start | bytes 184328 | tf_op jit(solution)/shard_map/ppermute | solution.py:497
  26.7 4.0 %collective-permute-start.7 = (f32[72,128]{1,0:T(8,128)S(1)}, f32[72,128]{1,0:T(8,128)S(1)}, u32[]{:S(2)}, u32[]{:S(2)}) collective-permute-start(f32[72,128]{1,0:T(8,128)S(1)} %hand_on.3), channel_id=1, source_target_pairs={{0,2},{1,3},{2,0},{3,1},{4,6},{5,7},{6,4},{7,5},{8,10},{9,11},{10,... | collective-permute-start | bytes 110600 | tf_op jit(solution)/shard_map/ppermute | solution.py:506
